TPU v7x, 32 devices: a whole 2x2x4 slice. The times are simulated.
32 devices in a mesh: groups: 2 (over x), seqt: 16 (over z, y, core).
Axes of the slice: x: 2, y: 2, z: 4, core: 2. Of those that a mesh axis runs over, the one named last changes fastest.
Arguments:
- out_grad: bfloat16 [4096, 4096], P(('groups', 'seqt')), parts along dimension 0, may hold values from -6 to 6
- hidden: bfloat16 [4096, 16384], P(('groups', 'seqt')), parts along dimension 0, may hold values from -0.13183594 to 0.13183594
- down_tiles: bfloat16 [128, 4, 128, 128], P('seqt'), may hold values from -0.3125 to 0.3125
- row_blocks: int32 [16, 4], replicated, may hold values from 0 to 31, as said below
- tile_mask: int32 [128, 4], P('seqt'), may hold values 0 or 1
Outputs:
- grad_hidden: bfloat16 [4096, 16384], P(('groups', 'seqt')), parts along dimension 0
- grad_tiles: float32 [256, 4, 128, 128], P(('groups', 'seqt')), parts along dimension 0
There are 2 independent parts, one for each index of `groups`. A program takes and returns all parts, laid end to end along the dimension named above; an argument that names none is the same for every part. Nothing has to cross between parts.
Inputs may be any that keep to these rules, and one draw needn't show every extreme that they name: `row_blocks`: the 4 row blocks of one device are distinct.
All inputs are finite; a program needn't handle non-finite values. No bound on the sum of `tile_mask` on one device may be relied on, other than what follows from the above.
Results may differ from a plain program's by a relative error of at most 0.001.
Values may be sent and summed in bfloat16 or wider, within the bound.
A program may use at most 128 MiB of HBM per device.

v0:
```python
import jax
import jax.numpy as jnp
from jax import lax
from jax.sharding import PartitionSpec as P


def on_device(out_grad, hidden, down_tiles, row_blocks, tile_mask):
    devices = lax.axis_size("seqt")
    tok_rows = out_grad.shape[0]
    model_width = out_grad.shape[1]
    col_count = down_tiles.shape[0]
    slot_count = down_tiles.shape[1]
    tile_size = down_tiles.shape[2]
    grad_blocks = out_grad.reshape(tok_rows, model_width // tile_size, tile_size)
    picked = jnp.take(grad_blocks, row_blocks.reshape(-1), axis=1)
    picked = picked.reshape(tok_rows, devices * slot_count * tile_size)
    rows_in = lax.all_to_all(picked, "seqt", split_axis=1, concat_axis=0, tiled=True)
    columns_in = lax.all_to_all(hidden, "seqt", split_axis=1, concat_axis=0, tiled=True)
    mask_float = tile_mask.astype(jnp.float32)
    masked = down_tiles * tile_mask[:, :, None, None].astype(down_tiles.dtype)
    weight_mat = masked.transpose(0, 2, 1, 3).reshape(col_count * tile_size, slot_count * tile_size)
    grad_local = lax.dot_general(
        rows_in, weight_mat, (((1,), (1,)), ((), ())), preferred_element_type=jnp.float32
    )
    products = lax.dot_general(
        columns_in, rows_in, (((0,), (0,)), ((), ())), preferred_element_type=jnp.float32
    )
    grad_tiles = products.reshape(col_count, tile_size, slot_count, tile_size).transpose(0, 2, 1, 3)
    grad_tiles = grad_tiles * mask_float[:, :, None, None]
    returned = lax.all_to_all(
        grad_local.astype(jnp.bfloat16), "seqt", split_axis=0, concat_axis=1, tiled=True
    )
    return (returned, grad_tiles)


def solution(mesh):
    return jax.shard_map(
        on_device,
        mesh=mesh,
        in_specs=(
            P(("groups", "seqt"), None),
            P(("groups", "seqt"), None),
            P("seqt", None, None, None),
            P(),
            P("seqt", None),
        ),
        out_specs=(P(("groups", "seqt"), None), P(("groups", "seqt"), None, None, None)),
        check_vma=False,
    )
```

profile of v0, /device:TPU:17, one launch (start us, length us, event | category | flops | bytes accessed | tf_op | source)
XLA Modules:
  0.0 265.9 jit_solution(12979687123918837915)
XLA Ops:
  0.6 0.8 copy.26
  1.4 0.7 compare_and_fusion
  2.1 1.6 copy.25
  3.7 0.7 copy.27
  4.5 2.1 gather_fusion
  6.6 3.2 %copy.28 = bf16[128,64,128]{0,2,1:T(8,128)(2,1)S(1)} copy(bf16[128,64,128]{2,0,1:T(8,128)(2,1)} %bitcast.49) | data formatting | bytes 4194304 | tf_op jit(solution)/shard_map/jit(_take)/gather | solution.py:15
  10.0 2.6 bitcast_select_fusion
  12.7 6.5 %all-to-all-start = ((bf16[128,16,512]{0,2,1:T(8,128)(2,1)}), bf16[128,16,512]{0,2,1:T(8,128)(2,1)S(1)}, u32[]{:S(2)}, u32[]{:S(2)}) async-start(bf16[128,16,512]{0,2,1:T(8,128)(2,1)} %bitcast_select_fusion), calls=%async_computation | async-start | bytes 4194304 | tf_op jit(solution)/shard_map/all_to_all | solution.py:17
  19.2 6.4 %copy.33 = bf16[128,16384]{0,1:T(8,128)(2,1)} copy(bf16[128,16384]{1,0:T(8,128)(2,1)} %param.6) | data formatting | bytes 8388608 | tf_op args[1]
  25.5 6.5 %copy.34 = bf16[128,16,1024]{2,0,1:T(8,128)(2,1)} copy(bf16[128,16,1024]{0,2,1:T(8,128)(2,1)} %bitcast.46) | data formatting | bytes 8388608 | tf_op jit(solution)/shard_map/all_to_all | solution.py:18
  32.0 34.3 %all-to-all-done = bf16[128,16,512]{0,2,1:T(8,128)(2,1)S(1)} async-done(((bf16[128,16,512]{0,2,1:T(8,128)(2,1)}), bf16[128,16,512]{0,2,1:T(8,128)(2,1)S(1)}, u32[]{:S(2)}, u32[]{:S(2)}) %all-to-all-start) | async-done | bytes 2097184 | tf_op jit(solution)/shard_map/all_to_all | solution.py:17
  66.3 5.2 %all-to-all-start.2 = ((bf16[128,16,1024]{2,0,1:T(8,128)(2,1)}), bf16[128,16,1024]{2,0,1:T(8,128)(2,1)}, u32[]{:S(2)}, u32[]{:S(2)}) async-start(bf16[128,16,1024]{2,0,1:T(8,128)(2,1)} %copy.34), calls=%async_computation.2 | async-start | bytes 8388608 | tf_op jit(solution)/shard_map/all_to_all | solution.py:18
  71.6 1.4 multiply_bitcast_fusion.1
  73.0 1.4 copy.31
  74.4 2.6 copy.29
  77.0 6.0 %convolution_convert_fusion = bf16[2048,1024]{1,0:T(8,128)(2,1)} fusion(bf16[2048,512]{1,0:T(8,128)(2,1)} %bitcast.54, bf16[64,8,8,128]{3,2,1,0:T(8,128)(2,1)S(1)} %bitcast.55), kind=kOutput, calls=%fused_computation.3 | convolution fusion | flops 2149580800 | bytes 7340032 | tf_op jit(solution)/shard_map/dot_general | solution.py:22
  83.0 80.7 %all-to-all-done.2 = bf16[128,16,1024]{2,0,1:T(8,128)(2,1)} async-done(((bf16[128,16,1024]{2,0,1:T(8,128)(2,1)}), bf16[128,16,1024]{2,0,1:T(8,128)(2,1)}, u32[]{:S(2)}, u32[]{:S(2)}) %all-to-all-start.2) | async-done | bytes 4194336 | tf_op jit(solution)/shard_map/all_to_all | solution.py:18
  163.7 5.2 %all-to-all-start.1 = ((bf16[16,128,1024]{2,1,0:T(8,128)(2,1)}), bf16[16,128,1024]{2,1,0:T(8,128)(2,1)}, u32[]{:S(2)}, u32[]{:S(2)}) async-start(bf16[16,128,1024]{2,1,0:T(8,128)(2,1)} %bitcast.51), calls=%async_computation.1 | async-start | bytes 8388608 | tf_op jit(solution)/shard_map/all_to_all | solution.py:30
  169.0 4.1 %fusion.2 = f32[64,8,8,128]{3,1,2,0:T(8,128)S(1)} fusion(bf16[128,16,1024]{2,0,1:T(8,128)(2,1)} %all-to-all-done.2, bf16[128,16,512]{0,2,1:T(8,128)(2,1)S(1)} %all-to-all-done), kind=kOutput, calls=%fused_computation.6 | convolution fusion | flops 2147483648 | bytes 8388608 | tf_op jit(solution)/shard_map/dot_general | solution.py:25
  173.1 1.8 copy.40
  174.9 1.9 copy.36
  176.8 1.5 multiply_bitcast_fusion
  178.3 82.7 %all-to-all-done.1 = bf16[16,128,1024]{2,1,0:T(8,128)(2,1)} async-done(((bf16[16,128,1024]{2,1,0:T(8,128)(2,1)}), bf16[16,128,1024]{2,1,0:T(8,128)(2,1)}, u32[]{:S(2)}, u32[]{:S(2)}) %all-to-all-start.1) | async-done | bytes 4194336 | tf_op jit(solution)/shard_map/all_to_all | solution.py:30
  261.1 4.8 %copy.37 = bf16[16,16,8,1024]{3,2,0,1:T(8,128)(2,1)} copy(bf16[16,16,8,1024]{3,2,1,0:T(8,128)(2,1)} %bitcast.15) | data formatting | bytes 8388608 | tf_op jit(solution)/shard_map/all_to_all | solution.py:30
  (13 shorter events, 0.5 us)
Async XLA Ops:
  12.7 53.6 %all-to-all-start = ((bf16[128,16,512]{0,2,1:T(8,128)(2,1)}), bf16[128,16,512]{0,2,1:T(8,128)(2,1)S(1)}, u32[]{:S(2)}, u32[]{:S(2)}) async-start(bf16[128,16,512]{0,2,1:T(8,128)(2,1)} %bitcast_select_fusion), calls=%async_computation | async-start | bytes 4194304 | tf_op jit(solution)/shard_map/all_to_all | solution.py:17
  32.0 39.5 %copy-start.1 = (s32[8,4]{0,1:T(4,128)S(1)}, s32[8,4]{0,1:T(4,128)}, u32[]{:S(2)}) copy-start(s32[8,4]{0,1:T(4,128)} %param.9) | copy-start | bytes 388
  66.3 97.4 %all-to-all-start.2 = ((bf16[128,16,1024]{2,0,1:T(8,128)(2,1)}), bf16[128,16,1024]{2,0,1:T(8,128)(2,1)}, u32[]{:S(2)}, u32[]{:S(2)}) async-start(bf16[128,16,1024]{2,0,1:T(8,128)(2,1)} %copy.34), calls=%async_computation.2 | async-start | bytes 8388608 | tf_op jit(solution)/shard_map/all_to_all | solution.py:18
  74.4 2.6 copy-start
  163.7 97.4 %all-to-all-start.1 = ((bf16[16,128,1024]{2,1,0:T(8,128)(2,1)}), bf16[16,128,1024]{2,1,0:T(8,128)(2,1)}, u32[]{:S(2)}, u32[]{:S(2)}) async-start(bf16[16,128,1024]{2,1,0:T(8,128)(2,1)} %bitcast.51), calls=%async_computation.1 | async-start | bytes 8388608 | tf_op jit(solution)/shard_map/all_to_all | solution.py:30
where the time goes:
time: 267 us; the launch traced here: 266 us
  waiting for transfers between devices  198 us (74%)
  local copies, waits for them, and re-layouts  34.2 us (13%)
  starting transfers between devices  16.9 us (6%)
  matrix products  10.1 us (4%)
  other arithmetic  6.23 us (2%)
    all_to_all x1, waiting for transfers between devices, on_device(): lax.all_to_all(grad_local.astype(jnp.bfloat16), 'seqt', split_axis=0, con...  82.7 us
    all_to_all x1, waiting for transfers between devices, on_device(): lax.all_to_all(hidden, 'seqt', split_axis=1, concat_axis=0, tiled=True)  80.7 us
    all_to_all x1, waiting for transfers between devices, on_device(): lax.all_to_all(picked, 'seqt', split_axis=1, concat_axis=0, tiled=True)  34.3 us
    unnamed x9, local copies, waits for them, and re-layouts  10.5 us
    all_to_all x1, starting transfers between devices, on_device(): lax.all_to_all(picked, 'seqt', split_axis=1, concat_axis=0, tiled=True)  6.5 us
    all_to_all x1, local copies, waits for them, and re-layouts, on_device(): lax.all_to_all(hidden, 'seqt', split_axis=1, concat_axis=0, tiled=True)  6.45 us
    dot_general x1, matrix products, on_device(): lax.dot_general(rows_in, weight_mat, (((1,), (1,)), ((), ())), preferred_...  5.95 us
    gather x2, local copies, waits for them, and re-layouts, on_device(): picked = jnp.take(grad_blocks, row_blocks.reshape(-1), axis=1)  5.35 us
  transfers between devices with their start and end apart: 3, of which 3 were waited for; matrix products, arithmetic and copies ran while one was open for 13% of the time, Pallas kernels for 0%

commit v1 on v0

v1 whole, which is shorter than its diff:
```python
import functools

import jax
import jax.numpy as jnp
from jax import lax
from jax.experimental import pallas as pl
from jax.experimental.pallas import tpu as pltpu
from jax.sharding import PartitionSpec as P

MESH = pl.DeviceIdType.MESH


def prepare(rb, mask, og, tiles, picked, weight):
    n, slots = rb.shape
    cols, _, tile, _ = tiles.shape
    for d in range(n):
        for k in range(slots):
            at = pl.multiple_of(rb[d, k] * tile, tile)
            picked[d, :, k * tile : (k + 1) * tile] = og[:, pl.ds(at, tile)]
    for c in range(cols):
        for k in range(slots):
            kept = tiles[c, k].astype(jnp.float32) * mask[c, k].astype(jnp.float32)
            weight[k * tile : (k + 1) * tile, c * tile : (c + 1) * tile] = kept.T.astype(weight.dtype)


def kernel(
    groups, n, nz, ny,
    mask, hid, picked, weight, gh, gt,
    rows, hbuf, wbuf,
    hsend, hrecv, rsend, rrecv, wrecv, zsend, ysend, xsend, csend, own_sem,
):
    g, me = lax.axis_index("groups"), lax.axis_index("seqt")
    core = me % 2
    chip = me // 2
    y, z = chip % ny, chip // ny
    tok = hid.shape[0]
    cols, slots, tile, _ = gt.shape
    width = cols * tile
    depth = slots * tile
    share = depth // groups

    def dev(zz, yy, cc):
        return (zz * ny + yy) * 2 + cc

    barrier = pltpu.get_barrier_semaphore()
    for i in range(1, n):
        pl.semaphore_signal(barrier, 1, device_id=(g, (me + i) % n), device_id_type=MESH)
    for i in range(1, groups):
        pl.semaphore_signal(barrier, 1, device_id=((g + i) % groups, me), device_id_type=MESH)

    own_hidden = pltpu.make_async_copy(
        hid.at[:, pl.ds(me * width, width)], hbuf.at[pl.ds(me * tok, tok), :], own_sem
    )
    own_hidden.start()
    wbuf[me] = weight[...]
    pl.semaphore_wait(barrier, n - 1 + groups - 1)

    def w_copy(d, part, sem, to):
        ref = wbuf.at[d, pl.ds(part * share, share), :]
        return pltpu.make_async_remote_copy(
            ref, ref, send_sem=sem, recv_sem=wrecv.at[d, part], device_id=to, device_id_type=MESH
        )

    def z_copy(way, zz):
        step = 1 if way == 0 else -1
        return w_copy(dev(zz, y, core), g, zsend.at[way, zz], (g, dev(z + step, y, core)))

    def y_copy(zz):
        return w_copy(dev(zz, y, core), g, ysend.at[zz], (g, dev(z, 1 - y, core)))

    def x_copy(zz, yy, i):
        return w_copy(dev(zz, yy, core), g, xsend.at[zz * ny + yy, i], ((g + i) % groups, me))

    def c_copy(zz, yy):
        d = dev(zz, yy, core)
        return pltpu.make_async_remote_copy(
            wbuf.at[d], wbuf.at[d], send_sem=csend.at[zz * ny + yy], recv_sem=wrecv.at[d, 0],
            device_id=(g, dev(z, y, 1 - core)), device_id_type=MESH,
        )

    def h_copy(i):
        p = (me + i) % n
        return pltpu.make_async_remote_copy(
            hid.at[:, pl.ds(p * width, width)], hbuf.at[pl.ds(me * tok, tok), :],
            send_sem=hsend.at[i], recv_sem=hrecv.at[me], device_id=(g, p), device_id_type=MESH,
        )

    def r_copy(i):
        p = (me + i) % n
        return pltpu.make_async_remote_copy(
            picked.at[p], rows.at[pl.ds(me * tok, tok), :],
            send_sem=rsend.at[i], recv_sem=rrecv.at[me], device_id=(g, p), device_id_type=MESH,
        )

    pl.when(z < nz - 1)(lambda: z_copy(0, z).start())
    pl.when(z > 0)(lambda: z_copy(1, z).start())
    if ny > 1:
        y_copy(z).start()
    c_copy(z, y).start()

    order = sorted(range(1, n), key=lambda i: abs(i - n // 2))
    for i in order:
        h_copy(i).start()
        r_copy(i).start()
    rows[pl.ds(me * tok, tok), :] = picked[me]
    gt[...] = jnp.zeros_like(gt)

    def to_groups(zz, yy):
        for i in range(1, groups):
            x_copy(zz, yy, i).start()

    def z_arrival(s, way):
        zz = z - s if way == 0 else z + s
        fits = (zz >= 0) if way == 0 else (zz < nz)
        more = (z < nz - 1) if way == 0 else (z > 0)

        @pl.when(fits)
        def _():
            w_copy(dev(zz, y, core), g, own_sem, (g, dev(z, y, 1 - core))).wait_recv()
            pl.when(more)(lambda: z_copy(way, zz).start())
            if ny > 1:
                y_copy(zz).start()
            to_groups(zz, y)

    def y_arrival(s, way):
        zz = z - s if way == 0 else z + s
        fits = (zz >= 0) if way == 0 else (zz < nz)

        @pl.when(fits)
        def _():
            w_copy(dev(zz, 1 - y, core), g, own_sem, (g, dev(z, y, 1 - core))).wait_recv()
            to_groups(zz, 1 - y)

    def x_arrival(s, way, yy):
        zz = z - s if way == 0 else z + s
        fits = (zz >= 0) if way == 0 else (zz < nz)

        @pl.when(fits)
        def _():
            for i in range(1, groups):
                w_copy(dev(zz, yy, core), (g + i) % groups, own_sem, (g, dev(z, y, 1 - core))).wait_recv()
            c_copy(zz, yy).start()

    def multiply(d):
        piece = min(width, 512)
        for c in range(width // piece):
            w = wbuf[d, :, c * piece : (c + 1) * piece]
            out = jnp.dot(picked[d], w, preferred_element_type=jnp.float32).astype(gh.dtype)
            gh[:, pl.ds(pl.multiple_of(d * width + c * piece, 128), piece)] = out

    def ways(s):
        return (0,) if s == 0 else (0, 1)

    for s in range(nz + 2):
        if 1 <= s < nz:
            for way in ways(s):
                z_arrival(s, way)
        if ny > 1 and 0 <= s - 1 < nz:
            for way in ways(s - 1):
                y_arrival(s - 1, way)
        if 0 <= s - 2 < nz:
            for way in ways(s - 2):
                if s - 2 > 0:
                    x_arrival(s - 2, way, y)
                if ny > 1:
                    x_arrival(s - 2, way, 1 - y)

    @pl.loop(0, n // 2)
    def _(j):
        multiply(j * 2 + core)

    own_hidden.wait()
    block = min(width, 256)

    @pl.loop(0, n // 2)
    def _(j):
        other = (chip + j) % (n // 2)
        for c in range(2):
            src = other * 2 + c

            @pl.when(src != me)
            def _():
                at = pl.ds(src * tok, tok)
                pltpu.make_async_remote_copy(
                    hbuf.at[at, :], hbuf.at[at, :], send_sem=own_sem, recv_sem=hrecv.at[src],
                    device_id=(g, dev(z, y, 1 - core)), device_id_type=MESH,
                ).wait_recv()
                pltpu.make_async_remote_copy(
                    rows.at[at, :], rows.at[at, :], send_sem=own_sem, recv_sem=rrecv.at[src],
                    device_id=(g, dev(z, y, 1 - core)), device_id_type=MESH,
                ).wait_recv()

        at = pl.ds(pl.multiple_of(other * 2 * tok, 2 * tok), 2 * tok)

        @pl.loop(0, width // block)
        def _(b):
            h = hbuf[at, pl.ds(pl.multiple_of(b * block, block), block)]
            prod = lax.dot_general(
                h, rows[at, :], (((0,), (0,)), ((), ())), preferred_element_type=jnp.float32
            )
            for c in range(block // tile):
                for k in range(slots):
                    part = prod[c * tile : (c + 1) * tile, k * tile : (k + 1) * tile]
                    gt[b * (block // tile) + c, k] += part

    for c in range(cols):
        for k in range(slots):
            gt[c, k] = gt[c, k] * mask[c, k].astype(jnp.float32)

    @pl.loop(0, n // 2)
    def _(j):
        d = j * 2 + 1 - core
        pltpu.make_async_remote_copy(
            wbuf.at[d], wbuf.at[d], send_sem=own_sem, recv_sem=wrecv.at[d, 0],
            device_id=(g, dev(z, y, 1 - core)), device_id_type=MESH,
        ).wait_recv()
        multiply(d)

    for i in range(1, n):
        h_copy(i).wait_send()
        r_copy(i).wait_send()
    for s in range(nz):
        for way in ways(s):
            for go in (0, 1) if s == 0 else (way,):
                zz = z - s if way == 0 else z + s
                fits = (zz >= 0) if way == 0 else (zz < nz)
                more = (z < nz - 1) if go == 0 else (z > 0)
                pl.when(fits & more)(functools.partial(lambda go, zz: z_copy(go, zz).wait_send(), go, zz))
    for zz in range(nz):
        if ny > 1:
            y_copy(zz).wait_send()
        for yy in range(ny):
            c_copy(zz, yy).wait_send()

            @pl.when((zz != z) | (yy != y))
            def _():
                for i in range(1, groups):
                    x_copy(zz, yy, i).wait_send()


def solution(mesh):
    groups, n = mesh.shape["groups"], mesh.shape["seqt"]
    nz = groups * n // 8
    ny = n // 2 // nz

    def on_device(out_grad, hidden, down_tiles, row_blocks, tile_mask):
        tok, ff = hidden.shape
        cols, slots, tile, _ = down_tiles.shape
        width, depth = cols * tile, slots * tile
        dma = pltpu.SemaphoreType.DMA
        vmem = pl.BlockSpec(memory_space=pltpu.VMEM)
        smem = pl.BlockSpec(memory_space=pltpu.SMEM)
        n_rows = row_blocks.shape[0]
        picked, weight = pl.pallas_call(
            prepare,
            out_shape=(
                jax.ShapeDtypeStruct((n_rows, tok, depth), jnp.bfloat16),
                jax.ShapeDtypeStruct((depth, width), jnp.bfloat16),
            ),
            in_specs=[smem, smem, vmem, vmem],
            out_specs=(vmem, vmem),
            compiler_params=pltpu.CompilerParams(vmem_limit_bytes=40 << 20),
        )(row_blocks, tile_mask, out_grad, down_tiles)
        return tuple(pl.pallas_call(
            functools.partial(kernel, groups, n, nz, ny),
            out_shape=(
                jax.ShapeDtypeStruct((tok, ff), jnp.bfloat16),
                jax.ShapeDtypeStruct((cols, slots, tile, tile), jnp.float32),
            ),
            in_specs=[smem, pl.BlockSpec(memory_space=pl.ANY), vmem, vmem],
            out_specs=(vmem, vmem),
            scratch_shapes=[
                pltpu.VMEM((n * tok, depth), jnp.bfloat16),
                pltpu.VMEM((n * tok, width), jnp.bfloat16),
                pltpu.VMEM((n, depth, width), jnp.bfloat16),
                dma((n,)), dma((n,)), dma((n,)), dma((n,)), dma((n, groups)),
                dma((2, nz)), dma((nz,)), dma((nz * ny, groups)), dma((nz * ny,)), dma(()),
            ],
            compiler_params=pltpu.CompilerParams(
                collective_id=0, has_side_effects=True, vmem_limit_bytes=56 << 20
            ),
            cost_estimate=pl.CostEstimate(
                flops=4 * n * tok * depth * width, bytes_accessed=20 << 20, transcendentals=0
            ),
        )(tile_mask, hidden, picked, weight))

    return jax.shard_map(
        on_device,
        mesh=mesh,
        in_specs=(
            P(("groups", "seqt"), None),
            P(("groups", "seqt"), None),
            P("seqt", None, None, None),
            P(),
            P("seqt", None),
        ),
        out_specs=(P(("groups", "seqt"), None), P(("groups", "seqt"), None, None, None)),
        check_vma=False,
    )
```

time: 267 us -> 247 us (0.925); the launches traced: 266 us -> 243 us
  Pallas kernels: 0 us -> 230 us
  waiting for transfers between devices: 198 us -> 0 us
  local copies, waits for them, and re-layouts: 34.2 us -> 12.3 us
  starting transfers between devices: 16.9 us -> 0 us
  matrix products: 10.1 us -> 0 us
  other arithmetic: 6.23 us -> 0 us
    pallas_call x0 -> x2, Pallas kernels: none -> 230 us  [the longest x1 228 us: on_device(): pl.pallas_call(functools.partial(kernel, groups, n, nz, ny), out_shape=(j...]
    all_to_all x3 -> x0, waiting for transfers between devices: 198 us -> none  [the longest x1 82.7 us: on_device(): lax.all_to_all(grad_local.astype(jnp.bfloat16), 'seqt', split_axis=0, con...]
    all_to_all x3 -> x0, starting transfers between devices: 16.9 us -> none  [the longest x1 6.5 us: on_device(): lax.all_to_all(picked, 'seqt', split_axis=1, concat_axis=0, tiled=True)]
    all_to_all x3 -> x0, local copies, waits for them, and re-layouts: 13.9 us -> none  [the longest x1 6.45 us: on_device(): lax.all_to_all(hidden, 'seqt', split_axis=1, concat_axis=0, tiled=True)]
    dot_general x2 -> x0, matrix products: 10.1 us -> none  [the longest x1 5.95 us: on_device(): lax.dot_general(rows_in, weight_mat, (((1,), (1,)), ((), ())), preferred_...]
    gather x2 -> x0, local copies, waits for them, and re-layouts: 5.35 us -> none  [on_device(): picked = jnp.take(grad_blocks, row_blocks.reshape(-1), axis=1)]
    reshape x3 -> x0, local copies, waits for them, and re-layouts: 2.68 us -> none  [the longest x1 1.93 us: on_device(): products.reshape(col_count, tile_size, slot_count, tile_size)]
    unnamed x9 -> x16, local copies, waits for them, and re-layouts: 10.5 us -> 12.3 us
  transfers between devices with their start and end apart: 3 -> 0, of which waited for: 3 -> 0; matrix products, arithmetic and copies ran while one was open for 13% -> 0% of each run, Pallas kernels for 0% -> 0%
where the time goes in v1:
time: 247 us; the launch traced here: 243 us
  Pallas kernels  230 us (93%)
  local copies, waits for them, and re-layouts  12.3 us (5%)
    pallas_call x1, Pallas kernels, on_device(): pl.pallas_call(functools.partial(kernel, groups, n, nz, ny), out_shape=(j...  228 us
    unnamed x16, local copies, waits for them, and re-layouts  12.3 us

profile of v1, /device:TPU:17, one launch (start us, length us, event | category | flops | bytes accessed | tf_op | source)
XLA Modules:
  0.0 242.6 jit_solution(16712337218653956041)
XLA Ops:
  0.6 0.8 copy.9.mask
  1.4 0.0 copy-start.2
  1.4 0.8 copy.7.rb
  2.1 0.0 copy-start
  2.2 1.2 copy-done
  3.4 0.0 copy-start.1
  3.4 1.2 copy-done.1
  4.6 1.6 shard_map.68
  6.2 0.0 copy-start.3
  6.2 1.3 copy-done.3
  7.5 0.0 copy-start.4
  7.5 1.0 copy-done.4
  8.5 0.0 copy-done.2
  8.5 228.1 %shard_map.69 = (bf16[128,16384]{1,0:T(8,128)(2,1)}, f32[8,4,128,128]{3,2,1,0:T(8,128)}) custom-call(s32[8,4]{1,0:T(8,128)} %copy-done.2, bf16[128,16384]{1,0:T(8,128)(2,1)} %hid.1, bf16[16,128,512]{2,1,0:T(8,128)(2,1)} %copy-done.3, bf16[512,1024]{1,0:T(8,128)(2,1)} %copy-done.4), custom_call_target="tpu_custom_call" | custom-call | flops 4294967296 | bytes 20971520 | tf_op jit(solution)/shard_map/pallas_call | solution.py:264
  236.5 0.0 copy-start.5
  236.6 4.7 %copy.12 = bf16[128,16384]{1,0:T(8,128)(2,1)} copy(bf16[128,16384]{1,0:T(8,128)(2,1)} %get-tuple-element.8) | data formatting | bytes 8388608
  241.3 0.0 copy-done.5
  241.3 1.3 copy.13
Async XLA Ops:
  1.4 7.1 %copy-start.2 = (s32[8,4]{1,0:T(8,128)}, s32[8,4]{1,0:T(8,128)S(1)}, u32[]{:S(2)}) copy-start(s32[8,4]{1,0:T(8,128)S(1)} %copy.9.mask) | copy-start | bytes 388
  2.1 1.2 copy-start
  3.4 1.2 copy-start.1
  6.2 1.3 copy-start.3
  7.5 1.0 copy-start.4
  236.5 4.7 %copy-start.5 = (f32[8,4,128,128]{3,2,1,0:T(8,128)S(1)}, f32[8,4,128,128]{3,2,1,0:T(8,128)}, u32[]{:S(2)}) copy-start(f32[8,4,128,128]{3,2,1,0:T(8,128)} %get-tuple-element.9) | copy-start | bytes 6291460

commit v2 on v1

--- a/solution.py
+++ b/solution.py
@@ -21,6 +21,15 @@
         for k in range(slots):
             kept = tiles[c, k].astype(jnp.float32) * mask[c, k].astype(jnp.float32)
             weight[k * tile : (k + 1) * tile, c * tile : (c + 1) * tile] = kept.T.astype(weight.dtype)
+
+
+FIRST, EACH = 3, 2
+
+
+def send_order(n, nz):
+    line = n // nz
+    far = sorted(range(nz), key=lambda r: abs(2 * r - nz))
+    return [0] + [i for q in range(line) for i in (line * r + q for r in far) if i]
 
 
 def kernel(
@@ -48,8 +57,9 @@
     for i in range(1, groups):
         pl.semaphore_signal(barrier, 1, device_id=((g + i) % groups, me), device_id_type=MESH)
 
+    order = send_order(n, nz)
     own_hidden = pltpu.make_async_copy(
-        hid.at[:, pl.ds(me * width, width)], hbuf.at[pl.ds(me * tok, tok), :], own_sem
+        hid.at[:, pl.ds(me * width, width)], hbuf.at[pl.ds(0, tok), :], own_sem
     )
     own_hidden.start()
     wbuf[me] = weight[...]
@@ -78,19 +88,24 @@
             device_id=(g, dev(z, y, 1 - core)), device_id_type=MESH,
         )
 
-    def h_copy(i):
-        p = (me + i) % n
+    def h_copy(q):
+        p = (me + order[q]) % n
         return pltpu.make_async_remote_copy(
-            hid.at[:, pl.ds(p * width, width)], hbuf.at[pl.ds(me * tok, tok), :],
-            send_sem=hsend.at[i], recv_sem=hrecv.at[me], device_id=(g, p), device_id_type=MESH,
+            hid.at[:, pl.ds(p * width, width)], hbuf.at[pl.ds(q * tok, tok), :],
+            send_sem=hsend.at[q], recv_sem=hrecv.at[q], device_id=(g, p), device_id_type=MESH,
         )
 
-    def r_copy(i):
-        p = (me + i) % n
+    def r_copy(q):
+        p = (me + order[q]) % n
         return pltpu.make_async_remote_copy(
-            picked.at[p], rows.at[pl.ds(me * tok, tok), :],
-            send_sem=rsend.at[i], recv_sem=rrecv.at[me], device_id=(g, p), device_id_type=MESH,
+            picked.at[p], rows.at[pl.ds(q * tok, tok), :],
+            send_sem=rsend.at[q], recv_sem=rrecv.at[q], device_id=(g, p), device_id_type=MESH,
         )
+
+    def send(first, last):
+        for q in range(max(first, 1), min(last, n)):
+            h_copy(q).start()
+            r_copy(q).start()
 
     pl.when(z < nz - 1)(lambda: z_copy(0, z).start())
     pl.when(z > 0)(lambda: z_copy(1, z).start())
@@ -98,11 +113,8 @@
         y_copy(z).start()
     c_copy(z, y).start()
 
-    order = sorted(range(1, n), key=lambda i: abs(i - n // 2))
-    for i in order:
-        h_copy(i).start()
-        r_copy(i).start()
-    rows[pl.ds(me * tok, tok), :] = picked[me]
+    send(0, FIRST * n // 16)
+    rows[pl.ds(0, tok), :] = picked[me]
     gt[...] = jnp.zeros_like(gt)
 
     def to_groups(zz, yy):
@@ -140,6 +152,7 @@
             for i in range(1, groups):
                 w_copy(dev(zz, yy, core), (g + i) % groups, own_sem, (g, dev(z, y, 1 - core))).wait_recv()
             c_copy(zz, yy).start()
+            multiply(dev(zz, yy, core))
 
     def multiply(d):
         piece = min(width, 512)
@@ -151,8 +164,45 @@
     def ways(s):
         return (0,) if s == 0 else (0, 1)
 
-    for s in range(nz + 2):
-        if 1 <= s < nz:
+    def c_arrival(s, way, yy):
+        zz = z - s if way == 0 else z + s
+        fits = (zz >= 0) if way == 0 else (zz < nz)
+
+        @pl.when(fits)
+        def _():
+            d = dev(zz, yy, 1 - core)
+            pltpu.make_async_remote_copy(
+                wbuf.at[d], wbuf.at[d], send_sem=own_sem, recv_sem=wrecv.at[d, 0],
+                device_id=(g, dev(z, y, 1 - core)), device_id_type=MESH,
+            ).wait_recv()
+            multiply(d)
+
+    block = min(width, 256)
+
+    def accumulate(first):
+        for q in (first, first + 1):
+            if q == 0:
+                own_hidden.wait()
+            else:
+                h_copy(q).wait_recv()
+                r_copy(q).wait_recv()
+        at = pl.ds(first * tok, 2 * tok)
+
+        @pl.loop(0, width // block)
+        def _(b):
+            h = hbuf[at, pl.ds(pl.multiple_of(b * block, block), block)]
+            prod = lax.dot_general(
+                h, rows[at, :], (((0,), (0,)), ((), ())), preferred_element_type=jnp.float32
+            )
+            for c in range(block // tile):
+                for k in range(slots):
+                    part = prod[c * tile : (c + 1) * tile, k * tile : (k + 1) * tile]
+                    gt[b * (block // tile) + c, k] += part
+
+    done = 0
+    for s in range(1, nz + 4):
+        send((FIRST + (s - 1) * EACH) * n // 16, (FIRST + s * EACH) * n // 16 if s < nz + 3 else n)
+        if s < nz:
             for way in ways(s):
                 z_arrival(s, way)
         if ny > 1 and 0 <= s - 1 < nz:
@@ -164,57 +214,20 @@
                     x_arrival(s - 2, way, y)
                 if ny > 1:
                     x_arrival(s - 2, way, 1 - y)
-
-    @pl.loop(0, n // 2)
-    def _(j):
-        multiply(j * 2 + core)
-
-    own_hidden.wait()
-    block = min(width, 256)
-
-    @pl.loop(0, n // 2)
-    def _(j):
-        other = (chip + j) % (n // 2)
-        for c in range(2):
-            src = other * 2 + c
-
-            @pl.when(src != me)
-            def _():
-                at = pl.ds(src * tok, tok)
-                pltpu.make_async_remote_copy(
-                    hbuf.at[at, :], hbuf.at[at, :], send_sem=own_sem, recv_sem=hrecv.at[src],
-                    device_id=(g, dev(z, y, 1 - core)), device_id_type=MESH,
-                ).wait_recv()
-                pltpu.make_async_remote_copy(
-                    rows.at[at, :], rows.at[at, :], send_sem=own_sem, recv_sem=rrecv.at[src],
-                    device_id=(g, dev(z, y, 1 - core)), device_id_type=MESH,
-                ).wait_recv()
-
-        at = pl.ds(pl.multiple_of(other * 2 * tok, 2 * tok), 2 * tok)
-
-        @pl.loop(0, width // block)
-        def _(b):
-            h = hbuf[at, pl.ds(pl.multiple_of(b * block, block), block)]
-            prod = lax.dot_general(
-                h, rows[at, :], (((0,), (0,)), ((), ())), preferred_element_type=jnp.float32
-            )
-            for c in range(block // tile):
-                for k in range(slots):
-                    part = prod[c * tile : (c + 1) * tile, k * tile : (k + 1) * tile]
-                    gt[b * (block // tile) + c, k] += part
+        if s == 1:
+            multiply(me)
+        ready = n if s == nz + 3 else max(0, (FIRST + (s - 2) * EACH) * n // 16)
+        while done + 2 <= min(ready, n):
+            accumulate(done)
+            done += 2
+        if 0 <= s - 3 < nz:
+            for way in ways(s - 3):
+                for yy in ((y, 1 - y) if ny > 1 else (y,)):
+                    c_arrival(s - 3, way, yy)
 
     for c in range(cols):
         for k in range(slots):
             gt[c, k] = gt[c, k] * mask[c, k].astype(jnp.float32)
-
-    @pl.loop(0, n // 2)
-    def _(j):
-        d = j * 2 + 1 - core
-        pltpu.make_async_remote_copy(
-            wbuf.at[d], wbuf.at[d], send_sem=own_sem, recv_sem=wrecv.at[d, 0],
-            device_id=(g, dev(z, y, 1 - core)), device_id_type=MESH,
-        ).wait_recv()
-        multiply(d)
 
     for i in range(1, n):
         h_copy(i).wait_send()

time: 247 us -> 203 us (0.82)
  Pallas kernels: 230 us -> 187 us
    pallas_call x1, Pallas kernels: 228 us -> 186 us  [on_device(): pl.pallas_call(functools.partial(kernel, groups, n, nz, ny), out_shape=(j...]
where the time goes in v2:
time: 203 us; the launch traced here: 200 us
  Pallas kernels  187 us (92%)
  local copies, waits for them, and re-layouts  12.3 us (6%)
    pallas_call x1, Pallas kernels, on_device(): pl.pallas_call(functools.partial(kernel, groups, n, nz, ny), out_shape=(j...  186 us
    unnamed x16, local copies, waits for them, and re-layouts  12.3 us

profile of v2, /device:TPU:17, one launch (start us, length us, event | category | flops | bytes accessed | tf_op | source)
XLA Modules:
  0.0 200.1 jit_solution(3164084619183159487)
XLA Ops:
  0.6 0.8 copy.9.mask
  1.4 0.0 copy-start.2
  1.4 0.8 copy.7.rb
  2.1 0.0 copy-start
  2.2 1.2 copy-done
  3.4 0.0 copy-start.1
  3.4 1.2 copy-done.1
  4.6 1.6 shard_map.68
  6.2 0.0 copy-start.3
  6.2 1.3 copy-done.3
  7.5 0.0 copy-start.4
  7.5 1.0 copy-done.4
  8.5 0.0 copy-done.2
  8.5 185.5 %shard_map.69 = (bf16[128,16384]{1,0:T(8,128)(2,1)}, f32[8,4,128,128]{3,2,1,0:T(8,128)}) custom-call(s32[8,4]{1,0:T(8,128)} %copy-done.2, bf16[128,16384]{1,0:T(8,128)(2,1)} %hid.1, bf16[16,128,512]{2,1,0:T(8,128)(2,1)} %copy-done.3, bf16[512,1024]{1,0:T(8,128)(2,1)} %copy-done.4), custom_call_target="tpu_custom_call" | custom-call | flops 4294967296 | bytes 20971520 | tf_op jit(solution)/shard_map/pallas_call | solution.py:277
  194.0 0.0 copy-start.5
  194.0 4.7 %copy.12 = bf16[128,16384]{1,0:T(8,128)(2,1)} copy(bf16[128,16384]{1,0:T(8,128)(2,1)} %get-tuple-element.8) | data formatting | bytes 8388608
  198.7 0.0 copy-done.5
  198.7 1.3 copy.13
Async XLA Ops:
  1.4 7.1 %copy-start.2 = (s32[8,4]{1,0:T(8,128)}, s32[8,4]{1,0:T(8,128)S(1)}, u32[]{:S(2)}) copy-start(s32[8,4]{1,0:T(8,128)S(1)} %copy.9.mask) | copy-start | bytes 388
  2.1 1.2 copy-start
  3.4 1.2 copy-start.1
  6.2 1.3 copy-start.3
  7.5 1.0 copy-start.4
  194.0 4.7 %copy-start.5 = (f32[8,4,128,128]{3,2,1,0:T(8,128)S(1)}, f32[8,4,128,128]{3,2,1,0:T(8,128)}, u32[]{:S(2)}) copy-start(f32[8,4,128,128]{3,2,1,0:T(8,128)} %get-tuple-element.9) | copy-start | bytes 6291460

commit v3 on v2

--- a/solution.py
+++ b/solution.py
@@ -23,7 +23,7 @@
             weight[k * tile : (k + 1) * tile, c * tile : (c + 1) * tile] = kept.T.astype(weight.dtype)
 
 
-FIRST, EACH = 3, 2
+FIRST, EACH = 2, 3
 
 
 def send_order(n, nz):

time: 203 us -> 193 us (0.951); the launches traced: 200 us -> 193 us
  Pallas kernels: 187 us -> 180 us
    pallas_call x1, Pallas kernels: 186 us -> 179 us  [on_device(): pl.pallas_call(functools.partial(kernel, groups, n, nz, ny), out_shape=(j...]
where the time goes in v3:
time: 193 us
  Pallas kernels  180 us (93%)
  local copies, waits for them, and re-layouts  12.3 us (6%)
    pallas_call x1, Pallas kernels, on_device(): pl.pallas_call(functools.partial(kernel, groups, n, nz, ny), out_shape=(j...  179 us
    unnamed x16, local copies, waits for them, and re-layouts  12.3 us

profile of v3, /device:TPU:17, one launch (start us, length us, event | category | flops | bytes accessed | tf_op | source)
XLA Modules:
  0.0 193.2 jit_solution(7071899581781782619)
XLA Ops:
  0.6 0.8 copy.9.mask
  1.4 0.0 copy-start.2
  1.4 0.8 copy.7.rb
  2.1 0.0 copy-start
  2.2 1.2 copy-done
  3.4 0.0 copy-start.1
  3.4 1.2 copy-done.1
  4.6 1.6 shard_map.68
  6.2 0.0 copy-start.3
  6.2 1.3 copy-done.3
  7.5 0.0 copy-start.4
  7.5 1.0 copy-done.4
  8.5 0.0 copy-done.2
  8.5 178.7 %shard_map.69 = (bf16[128,16384]{1,0:T(8,128)(2,1)}, f32[8,4,128,128]{3,2,1,0:T(8,128)}) custom-call(s32[8,4]{1,0:T(8,128)} %copy-done.2, bf16[128,16384]{1,0:T(8,128)(2,1)} %hid.1, bf16[16,128,512]{2,1,0:T(8,128)(2,1)} %copy-done.3, bf16[512,1024]{1,0:T(8,128)(2,1)} %copy-done.4), custom_call_target="tpu_custom_call" | custom-call | flops 4294967296 | bytes 20971520 | tf_op jit(solution)/shard_map/pallas_call | solution.py:277
  187.1 0.0 copy-start.5
  187.2 4.7 %copy.12 = bf16[128,16384]{1,0:T(8,128)(2,1)} copy(bf16[128,16384]{1,0:T(8,128)(2,1)} %get-tuple-element.8) | data formatting | bytes 8388608
  191.9 0.0 copy-done.5
  191.9 1.3 copy.13
Async XLA Ops:
  1.4 7.1 %copy-start.2 = (s32[8,4]{1,0:T(8,128)}, s32[8,4]{1,0:T(8,128)S(1)}, u32[]{:S(2)}) copy-start(s32[8,4]{1,0:T(8,128)S(1)} %copy.9.mask) | copy-start | bytes 388
  2.1 1.2 copy-start
  3.4 1.2 copy-start.1
  6.2 1.3 copy-start.3
  7.5 1.0 copy-start.4
  187.1 4.7 %copy-start.5 = (f32[8,4,128,128]{3,2,1,0:T(8,128)S(1)}, f32[8,4,128,128]{3,2,1,0:T(8,128)}, u32[]{:S(2)}) copy-start(f32[8,4,128,128]{3,2,1,0:T(8,128)} %get-tuple-element.9) | copy-start | bytes 6291460
